TPU v7x, 256 devices: a whole 4x4x8 slice. The times are simulated.
256 devices in a mesh: dp: 32 (over z, y), ctx: 8 (over x, core).
Axes of the slice: x: 4, y: 4, z: 8, core: 2. Of those that a mesh axis runs over, the one named last changes fastest.
Arguments:
- uvqk: bfloat16 [32, 1024, 4096], P(None, 'ctx', 'dp'), may hold values from -1.5 to 1.5
- lengths: int32 [32], replicated, may hold values from 1 to 1024, as said below
- assignment: int32 [32], replicated, may hold values from 0 to 31, as said below
- buckets: int32 [1024], replicated, may hold values from 0 to 127
- rel_bias: float32 [8, 128], replicated, may hold values from -3 to 3
- cotangent: bfloat16 [32, 1024, 1024], P('dp', 'ctx'), may hold values from -6 to 6
Outputs:
- output: bfloat16 [32, 1024, 1024], P('dp', 'ctx')
- d_uvqk: bfloat16 [32, 1024, 4096], P(None, 'ctx', 'dp')
- d_bias: float32 [8, 128], replicated
Inputs may be any that keep to these rules, and one draw needn't show every extreme that they name: `lengths`: valid actions of each user; some user has exactly 1024. `assignment`: A permutation of the user ids. Slot d * 1 + t is the t-th slot of index d of dp; users are dealt to slots in order of falling length, alternating the direction over dp from one round to the next (with 1 = 1 there is a single round: slot d holds the user of rank d).
All inputs are finite; a program needn't handle non-finite values.
Results may differ from a plain program's by a relative error of at most 0.0055.
Values may be sent and summed in bfloat16 or wider, within the bound.
A program may use at most 128 MiB of HBM per device.

v0:
```python
import jax
import jax.numpy as jnp
from jax import lax
from jax.sharding import PartitionSpec as P


def diagonal_sums(plane):
    head_count, rows, columns = plane.shape
    padded = jnp.pad(plane, ((0, 0), (0, 0), (rows, 0)))
    flat = padded.reshape(head_count, rows * (columns + rows))
    flat = jnp.pad(flat, ((0, 0), (0, rows)))
    return flat.reshape(head_count, rows, columns + rows + 1).sum(1)


def on_device(uvqk, lengths, assignment, buckets, rel_bias, cotangent):
    users_all = assignment.shape[0]
    per_device = users_all // lax.axis_size("dp")
    dp_place = lax.axis_index("dp")
    ctx_place = lax.axis_index("ctx")
    arranged = jnp.take(uvqk, assignment, axis=0)
    gathered_local = lax.all_to_all(arranged, "dp", split_axis=0, concat_axis=2, tiled=True)
    local_rows = gathered_local.shape[1]
    feature_width = gathered_local.shape[2] // 4
    head_count, bucket_count = rel_bias.shape
    head_width = feature_width // head_count
    seq_total = buckets.shape[0]
    block_rows = min(512, seq_total)
    block_count = seq_total // block_rows
    slot_users = lax.dynamic_slice_in_dim(assignment, dp_place * per_device, per_device)
    user_len = jnp.take(lengths, slot_users)
    local_start = ctx_place * local_rows
    bucket_ids = jnp.arange(bucket_count, dtype=jnp.int32)
    onehot_table = (buckets[:, None] == bucket_ids[None, :]).astype(jnp.float32)
    relative = jnp.dot(rel_bias, onehot_table.T, precision=lax.Precision.HIGHEST)
    up_part = gathered_local[:, :, :feature_width]
    value_part = gathered_local[:, :, feature_width : 2 * feature_width]
    query_part = gathered_local[:, :, 2 * feature_width : 3 * feature_width]
    key_part = gathered_local[:, :, 3 * feature_width :]
    key_all, value_all = (
        lax.all_gather(key_part, "ctx", axis=1, tiled=True),
        lax.all_gather(value_part, "ctx", axis=1, tiled=True),
    )

    def split_heads(matrix):
        return matrix.reshape(matrix.shape[0], matrix.shape[1], head_count, head_width)

    def key_rows_of(block_index):
        start = block_index * block_rows
        key_block = key_all[:, start : start + block_rows]
        value_block = value_all[:, start : start + block_rows]
        return (start, key_block, value_block)

    attended = jnp.zeros((per_device, local_rows, head_count, head_width), jnp.float32)
    stored = []
    for block_index in range(block_count):
        start, key_block, value_block = key_rows_of(block_index)
        query_count = query_part.shape[1]
        key_count = key_block.shape[1]
        query_at = local_start + jnp.arange(query_count, dtype=jnp.int32)
        key_at = start + jnp.arange(key_count, dtype=jnp.int32)
        distance = query_at[:, None] - key_at[None, :]
        span = query_count + key_count - 1
        codes = jnp.clip(
            local_start - start + query_count - 1 - jnp.arange(span, dtype=jnp.int32),
            0,
            seq_total - 1,
        )
        vector = jnp.take(relative, codes, axis=1)
        flat = jnp.tile(vector, (1, query_count + 1))
        window = flat[:, query_count - 1 : query_count - 1 + query_count * (span - 1)]
        scores_score = (
            jnp.einsum(
                "bihd,bjhd->bhij",
                split_heads(query_part),
                split_heads(key_block),
                preferred_element_type=jnp.float32,
            )
            + window.reshape(head_count, query_count, span - 1)[:, :, :key_count][None]
        )
        query_live = query_at[None, :] < user_len[:, None]
        key_live = key_at[None, :] < user_len[:, None]
        scores_live = (distance >= 0)[None] & query_live[:, :, None] & key_live[:, None, :]
        score = scores_score
        live = scores_live[:, None]
        weight = jnp.where(live, score * jax.nn.sigmoid(score), 0.0).astype(jnp.bfloat16)
        attended = attended + jnp.einsum(
            "bhij,bjhd->bihd", weight, split_heads(value_block), preferred_element_type=jnp.float32
        )
        stored.append((score, live, weight))
    attended = attended.reshape(per_device, local_rows, feature_width)
    mean = attended.mean(-1, keepdims=True)
    centered = attended - mean
    variance = (centered * centered).mean(-1, keepdims=True)
    inverse_std = lax.rsqrt(variance + 1e-05)
    normed = centered * inverse_std
    gate_up = up_part.astype(jnp.float32)
    output = (normed * gate_up).astype(jnp.bfloat16)
    upstream = cotangent.astype(jnp.float32)
    grad_norm = upstream * gate_up
    d_up = (upstream * normed).astype(jnp.bfloat16)
    d_attended = (
        grad_norm
        - grad_norm.mean(-1, keepdims=True)
        - normed * (grad_norm * normed).mean(-1, keepdims=True)
    ) * inverse_std
    d_attended = d_attended.astype(jnp.bfloat16)
    d_query = jnp.zeros((per_device, local_rows, head_count, head_width), jnp.float32)
    d_bias = jnp.zeros((head_count, bucket_count), jnp.float32)
    diagonal_at = (
        local_start + local_rows - jnp.arange(block_rows + local_rows + 1, dtype=jnp.int32)
    )
    key_terms = []
    for block_index in range(block_count):
        start, key_block, value_block = key_rows_of(block_index)
        score, live, weight = stored[block_index]
        d_weight = jnp.einsum(
            "bihd,bjhd->bhij",
            split_heads(d_attended),
            split_heads(value_block),
            preferred_element_type=jnp.float32,
        )
        sigma = jax.nn.sigmoid(score)
        d_score = jnp.where(live, d_weight * sigma * (1.0 + score * (1.0 - sigma)), 0.0)
        d_score_b = d_score.astype(jnp.bfloat16)
        d_query = d_query + jnp.einsum(
            "bhij,bjhd->bihd", d_score_b, split_heads(key_block), preferred_element_type=jnp.float32
        )
        per_distance = diagonal_sums(d_score.sum(0))
        distance_codes = jnp.take(buckets, jnp.clip(diagonal_at - start, 0, seq_total - 1))
        distance_onehot = (distance_codes[:, None] == bucket_ids[None, :]).astype(jnp.float32)
        d_bias = d_bias + jnp.dot(per_distance, distance_onehot, precision=lax.Precision.HIGHEST)
        key_grad = jnp.einsum(
            "bhij,bihd->bjhd",
            d_score_b,
            split_heads(query_part),
            preferred_element_type=jnp.float32,
        )
        value_grad = jnp.einsum(
            "bhij,bihd->bjhd", weight, split_heads(d_attended), preferred_element_type=jnp.float32
        )
        key_terms.append(
            jnp.concatenate(
                [
                    key_grad.reshape(per_device, block_rows, feature_width),
                    value_grad.reshape(per_device, block_rows, feature_width),
                ],
                -1,
            )
        )
    summed = lax.psum_scatter(jnp.concatenate(key_terms, 1), "ctx", scatter_dimension=1, tiled=True)
    d_key = summed[:, :, :feature_width]
    d_value = summed[:, :, feature_width:]
    d_query = d_query.reshape(per_device, local_rows, feature_width)
    grads = jnp.concatenate(
        [
            d_up,
            d_value.astype(jnp.bfloat16),
            d_query.astype(jnp.bfloat16),
            d_key.astype(jnp.bfloat16),
        ],
        -1,
    )
    returned = lax.all_to_all(grads, "dp", split_axis=2, concat_axis=0, tiled=True)
    inverse_order = (
        jnp.zeros_like(assignment).at[assignment].set(jnp.arange(users_all, dtype=jnp.int32))
    )
    d_uvqk = jnp.take(returned, inverse_order, axis=0)
    d_bias = lax.psum(d_bias, ("dp", "ctx"))
    return (output, d_uvqk, d_bias)


def solution(mesh):
    in_specs = (P(None, "ctx", "dp"), P(), P(), P(), P(), P("dp", "ctx", None))
    out_specs = (P("dp", "ctx", None), P(None, "ctx", "dp"), P())
    return jax.shard_map(
        on_device, mesh=mesh, in_specs=in_specs, out_specs=out_specs, check_vma=False
    )
```

profile of v0, /device:TPU:1, one launch (start us, length us, event | category | flops | bytes accessed | tf_op | source)
XLA Modules:
  0.0 363.0 jit_solution(11632048348379219473)
XLA Ops:
  8.6 0.7 gather_fusion
  9.6 38.0 %all_to_all.36 = bf16[32,128,128]{2,1,0:T(8,128)(2,1)S(1)} all-to-all(bf16[32,128,128]{2,1,0:T(8,128)(2,1)S(1)} %broadcast_select_fusion.1), channel_id=1, replica_groups=mesh['dp'=32,'ctx'=8] {'dp'}, dimensions={0} | all-to-all | bytes 2097152 | tf_op jit(solution)/shard_map/all_to_all | solution.py:21
  48.3 0.9 fusion.26
  53.3 1.7 gather_fusion.2
  55.5 2.2 tile.21
  57.8 2.5 slice.88
  60.2 4.5 %reshape.556 = f32[8,128,638]{2,1,0:T(8,128)} reshape(f32[8,81664]{1,0:T(8,128)S(1)} %slice.88) | data formatting | bytes 5226496 | tf_op jit(solution)/shard_map/reshape | solution.py:78
  64.8 3.2 gather_fusion.1
  68.5 2.2 tile.9
  70.7 2.5 slice.84
  73.2 4.5 %reshape.553 = f32[8,128,638]{2,1,0:T(8,128)} reshape(f32[8,81664]{1,0:T(8,128)S(1)} %slice.84) | data formatting | bytes 5226496 | tf_op jit(solution)/shard_map/reshape | solution.py:78
  77.7 0.8 copy.72
  80.1 2.8 fusion.24
  82.9 2.2 select_convert_fusion.1
  85.1 26.4 %all-gather.3.cloned.1.call-done = bf16[1,1024,1024]{1,2,0:T(8,128)(2,1)} async-done(((bf16[1,128,1024]{1,2,0:T(8,128)(2,1)}), bf16[1,1024,1024]{1,2,0:T(8,128)(2,1)}) %all-gather.3.cloned.1.call-update) | async-done | bytes 2097168 | tf_op jit(solution)/shard_map/all_gather | solution.py:41
  111.5 1.8 fusion.25
  113.9 0.8 copy-done.8
  114.7 0.9 select_convert_fusion
  117.1 1.0 multiply_convert_fusion
  118.1 1.8 fusion.30
  119.9 1.7 fusion.31
  121.9 1.1 multiply_select_fusion.1
  123.0 1.1 multiply_select_fusion
  124.2 2.0 fusion.11
  126.1 1.7 fusion.7
  127.8 8.3 %maximum_maximum_fusion = f32[1,1024,2048]{1,2,0:T(8,128)} fusion(f32[1,512,1024]{1,2,0:T(8,128)} %bitcast.108, f32[1,512,1024]{1,2,0:T(8,128)} %bitcast.106, f32[1,512,1024]{1,2,0:T(8,128)} %bitcast.107, f32[1,512,1024]{1,2,0:T(8,128)} %bitcast.105), kind=kLoop, calls=%fused_computation.7 | loop fusion | flops 6291456 | bytes 16777216 | tf_op jit(solution)/shard_map/concatenate | solution.py:150
  136.7 1.1 copy-done.4
  138.5 52.9 %reduce-scatter.2.cloned.1.call-done = f32[1,128,2048]{1,2,0:T(8,128)} async-done(((f32[1,1024,2048]{1,2,0:T(8,128)}), f32[1,128,2048]{1,2,0:T(8,128)}) %reduce-scatter.2.cloned.1.call-update) | async-done | bytes 1048592 | tf_op jit(solution)/shard_map/reduce_scatter | solution.py:150
  191.3 1.3 convert.4
  192.8 17.1 %copy.92 = bf16[1,128,4096]{1,0,2:T(2,128)(2,1)} copy(bf16[1,128,4096]{1,2,0:T(8,128)(2,1)S(1)} %pad_maximum_fusion) | data formatting | bytes 2097152 | tf_op jit(solution)/shard_map/concatenate | solution.py:154
  210.3 23.4 %reduce.8 = bf16[4096,128]{1,0:T(8,128)(2,1)S(1)} reduce(bf16[4096,1,128]{2,1,0:T(2,128)(2,1)} %bitcast.104, bf16[]{:T(256)} %broadcast.366), dimensions={1}, to_apply=%bitcast.100.reduce_sub_computation | reduce | bytes 2097154
  233.8 1.1 reshape.671
  234.9 9.7 %all-to-all-start.1 = ((bf16[32,2,8192]{2,1,0:T(2,128)(2,1)}), bf16[32,2,8192]{2,1,0:T(2,128)(2,1)}, u32[]{:S(2)}, u32[]{:S(2)}) async-start(bf16[32,2,8192]{2,1,0:T(2,128)(2,1)} %reshape.671), calls=%async_computation.2 | async-start | bytes 2097152 | tf_op jit(solution)/shard_map/all_to_all | solution.py:163
  244.6 3.0 gather_fusion.4
  247.6 3.0 gather_fusion.5
  250.6 0.9 scatter_custom_fusion
  251.8 1.5 copy.89
  253.5 4.5 %reshape.564 = f32[8,128,641]{2,1,0:T(8,128)} reshape(f32[8,82048]{1,0:T(8,128)S(1)} %pad.15) | data formatting | bytes 5251072 | tf_op jit(solution)/shard_map/reshape | solution.py:12
  258.0 2.2 reduce_sum.66
  260.8 1.5 copy.90
  262.3 1.7 pad.17
  264.0 4.6 %reshape.566 = f32[8,128,641]{2,1,0:T(8,128)S(1)} reshape(f32[8,82048]{1,0:T(8,128)} %pad.17) | data formatting | bytes 5251072 | tf_op jit(solution)/shard_map/reshape | solution.py:12
  269.5 0.8 copy.79
  271.0 76.3 %psum.7 = f32[8,128]{1,0:T(8,128)} all-reduce(f32[8,128]{1,0:T(8,128)S(1)} %convolution_add_fusion.2), channel_id=1, replica_groups=mesh['dp'=32,'ctx'=8] {'dp','ctx'}, use_global_device_ids=true, to_apply=%region_8.12 | all-reduce | flops 1024 | bytes 8192 | tf_op jit(solution)/shard_map/psum | solution.py:168
  347.3 4.3 %reshape.672 = bf16[4096,1,128]{2,1,0:T(2,128)(2,1)S(1)} reshape(bf16[32,2,8192]{2,1,0:T(2,128)(2,1)} %all-to-all-done.1) | data formatting | bytes 2097152
  351.8 1.3 copy.78
  353.1 2.1 gather_fusion.3
  355.1 1.1 broadcast_select_fusion
  (103 shorter events, 12.9 us)
Async XLA Ops:
  7.2 1.5 copy-start
  7.2 72.9 %all-gather.5.cloned.1.call-start = ((), (), s32[]{:S(2)}) async-start(), calls=%async_computation.4 | async-start | bytes 2359296 | tf_op jit(solution)/shard_map/all_gather | solution.py:40
  47.6 2.5 copy-start.18
  47.6 5.0 %copy-start.2 = (s32[1024]{0:T(1024)S(1)}, s32[1024]{0:T(1024)}, u32[]{:S(2)}) copy-start(s32[1024]{0:T(1024)} %param.15) | copy-start | bytes 12292
  47.6 5.0 %copy-start.17 = (f32[8,128]{1,0:T(8,128)S(1)}, f32[8,128]{1,0:T(8,128)}, u32[]{:S(2)}) copy-start(f32[8,128]{1,0:T(8,128)} %param.16) | copy-start | bytes 12292
  48.3 6.9 %copy-start.6 = (bf16[1,128,32,128]{1,3,2,0:T(8,128)(2,1)}, bf16[1,128,32,128]{1,3,2,0:T(8,128)(2,1)S(1)}, u32[]{:S(2)}) copy-start(bf16[1,128,32,128]{1,3,2,0:T(8,128)(2,1)S(1)} %copy.63) | copy-start | bytes 3145732
  49.3 62.2 %all-gather.3.cloned.1.call-start = ((), (), s32[]{:S(2)}) async-start(), calls=%async_computation.3 | async-start | bytes 2359296 | tf_op jit(solution)/shard_map/all_gather | solution.py:41
  50.0 141.3 %reduce-scatter.2.cloned.1.call-start = ((), (), s32[]{:S(2)}) async-start(), calls=%async_computation.5 | async-start | bytes 9437184 | tf_op jit(solution)/shard_map/reduce_scatter | solution.py:150
  53.3 1.9 copy-start.13
  73.2 4.5 %copy-start.16 = (bf16[1,128,1024]{2,1,0:T(8,128)(2,1)S(1)}, bf16[1,128,1024]{2,1,0:T(8,128)(2,1)}, u32[]{:S(2)}) copy-start(bf16[1,128,1024]{2,1,0:T(8,128)(2,1)} %param.17) | copy-start | bytes 786436
  73.2 5.4 %copy-start.19 = (s32[32]{0:T(128)S(1)}, s32[32]{0:T(128)}, u32[]{:S(2)}) copy-start(s32[32]{0:T(128)} %param.13) | copy-start | bytes 388
  80.1 2.8 copy-start.11
  111.5 2.4 copy-start.10
  113.3 1.4 copy-start.8
  115.7 1.2 copy-start.7
  115.7 1.3 copy-start.12
  119.9 2.1 copy-start.20
  124.1 2.0 copy-start.3
  136.2 1.6 copy-start.4
  136.2 1.8 copy-start.9
  138.5 54.2 %copy-start.15 = (bf16[1,128,1024]{1,2,0:T(8,128)(2,1)S(1)}, bf16[1,128,1024]{1,2,0:T(8,128)(2,1)}, u32[]{:S(2)}) copy-start(bf16[1,128,1024]{1,2,0:T(8,128)(2,1)} %get-tuple-element.37) | copy-start | bytes 786436
  234.9 112.4 %all-to-all-start.1 = ((bf16[32,2,8192]{2,1,0:T(2,128)(2,1)}), bf16[32,2,8192]{2,1,0:T(2,128)(2,1)}, u32[]{:S(2)}, u32[]{:S(2)}) async-start(bf16[32,2,8192]{2,1,0:T(2,128)(2,1)} %reshape.671), calls=%async_computation.2 | async-start | bytes 2097152 | tf_op jit(solution)/shard_map/all_to_all | solution.py:163
  258.0 2.5 copy-start.5
  268.6 1.0 copy-start.14
  353.1 3.2 copy-start.1
Sparse Core Ops, SparseCore 0:
  49.4 29.4 all-gather.4
  80.7 30.7 all-gather.2
  136.3 55.0 reduce-scatter.1
where the time goes:
time: 369 us; the launch traced here: 363 us
  blocking collectives  114 us (31%)
  local copies, waits for them, and re-layouts  86 us (23%)
  waiting for transfers between devices  80 us (22%)
  other arithmetic  40.3 us (11%)
  between operations  17.2 us (5%)
  matrix products  15.4 us (4%)
  starting transfers between devices  9.82 us (3%)
    psum x1, blocking collectives, on_device(): d_bias = lax.psum(d_bias, ('dp', 'ctx'))  76.3 us
    reduce_scatter x1, waiting for transfers between devices, on_device(): lax.psum_scatter(jnp.concatenate(key_terms, 1), 'ctx', scatter_dimension=...  52.9 us
    all_to_all x1, blocking collectives, on_device(): lax.all_to_all(arranged, 'dp', split_axis=0, concat_axis=2, tiled=True)  38 us
    all_gather x1, waiting for transfers between devices, on_device(): lax.all_gather(value_part, 'ctx', axis=1, tiled=True)  26.4 us
    unnamed x1, other arithmetic  23.4 us
    concatenate x1, local copies, waits for them, and re-layouts, on_device(): jnp.concatenate([d_up, d_value.astype(jnp.bfloat16), d_query.astype(jnp.b...  17.1 us
    unnamed x52, local copies, waits for them, and re-layouts  15.5 us
    all_to_all x1, starting transfers between devices, on_device(): lax.all_to_all(grads, 'dp', split_axis=2, concat_axis=0, tiled=True)  9.7 us
  transfers between devices with their start and end apart: 4, of which 2 were waited for; matrix products, arithmetic and copies ran while one was open for 16% of the time, Pallas kernels for 0%

commit v1 on v0

v1 whole, which is shorter than its diff:
```python
import functools

import jax
import jax.numpy as jnp
from jax import lax
from jax.experimental import pallas as pl
from jax.experimental.pallas import tpu as pltpu
from jax.sharding import PartitionSpec as P

MESH = pl.DeviceIdType.MESH
TB = 256
W = 128
NN = (((1,), (0,)), ((), ()))
NT = (((1,), (1,)), ((), ()))


def mm(a, b, dims):
    return lax.dot_general(a, b, dims, preferred_element_type=jnp.float32)


def tile_at(ib, jb):
    return ib * (ib + 1) // 2 + jb


def kernel(
    H,
    U,
    assign,
    inverse,
    lengths,
    uvqk,
    cot,
    buckets,
    rel,
    out,
    grads,
    dbias,
    in_send,
    in_recv,
    cot_recv,
    out_send,
    g_send,
    g_recv,
    toep,
    wts,
    dsl,
    diag,
    vt,
    kt,
    ut,
    gt,
    at,
    dat,
    st_recv,
    st_send,
    db_send,
    db_recv,
    db_sum,
    db_all,
    s_in,
    r_in,
    s_cot,
    r_cot,
    s_st,
    r_st,
    s_out,
    r_out,
    s_g,
    r_g,
    s_db,
    r_db,
    s_dba,
    r_dba,
):
    k = lax.axis_index("dp")
    c = lax.axis_index("ctx")
    e = lax.rem(k, H)
    comp = lax.div(k, H)
    own = jnp.logical_and(e == c, True)
    LEN = H * W
    nt = LEN // TB
    per = TB // W

    def remote(src, dst, ss, rs, dev):
        return pltpu.make_async_remote_copy(
            src_ref=src, dst_ref=dst, send_sem=ss, recv_sem=rs, device_id=dev, device_id_type=MESH
        )

    barrier = pltpu.get_barrier_semaphore()

    def greet_slots(o, _):
        d = lax.rem(k + o, U)

        @pl.when(jnp.logical_not(jnp.logical_and(o == 0, own)))
        def _():
            pl.semaphore_signal(barrier, inc=1, device_id=(d, e), device_id_type=MESH)

        return 0

    lax.fori_loop(0, U, greet_slots, 0)

    def greet_owners(o, _):
        kk = lax.div(o, H) * H + c
        cc = lax.rem(o, H)

        @pl.when(jnp.logical_not(jnp.logical_and(kk == k, cc == c)))
        def _():
            pl.semaphore_signal(barrier, inc=1, device_id=(kk, cc), device_id_type=MESH)

        return 0

    lax.fori_loop(0, 4 * H, greet_owners, 0)

    def greet_ctx(o, _):
        pl.semaphore_signal(
            barrier, inc=1, device_id=(k, lax.rem(c + o, H)), device_id_type=MESH
        )
        return 0

    lax.fori_loop(1, H, greet_ctx, 0)

    def arrange(d, _):
        in_send[d] = uvqk[assign[d]]
        return 0

    lax.fori_loop(0, U, arrange, 0)

    pl.semaphore_wait(barrier, U + 4 * H + H - 1 - 2 * own.astype(jnp.int32))

    def in_copy(o):
        d = lax.rem(k + o, U)
        return remote(
            in_send.at[d],
            in_recv.at[comp, pl.ds(pl.multiple_of(c * W, W), W)],
            s_in.at[o],
            r_in.at[comp * H + c],
            (d, e),
        )

    def in_start(o, _):
        in_copy(o).start()
        return 0

    @pl.when(jnp.logical_not(own))
    def _():
        in_copy(0).start()

    @pl.when(own)
    def _():
        pltpu.make_async_copy(
            in_send.at[k],
            in_recv.at[comp, pl.ds(pl.multiple_of(c * W, W), W)],
            r_in.at[comp * H + c],
        ).start()

    lax.fori_loop(1, U, in_start, 0)

    def cot_copy(o):
        cc = lax.rem(c + o, H)
        return remote(
            cot.at[:, pl.ds(pl.multiple_of(cc * W, W), W)],
            cot_recv.at[pl.ds(pl.multiple_of(c * W, W), W)],
            s_cot.at[o],
            r_cot.at[c],
            (k, cc),
        )

    def cot_start(o, _):
        cot_copy(o).start()
        return 0

    lax.fori_loop(1, H, cot_start, 0)
    cot_recv[pl.ds(pl.multiple_of(c * W, W), W), :] = cot[:, pl.ds(pl.multiple_of(c * W, W), W)]

    eye = lax.broadcasted_iota(jnp.int32, (W, W), 0) == lax.broadcasted_iota(
        jnp.int32, (W, W), 1
    )
    onehot = lax.broadcasted_iota(jnp.int32, (W, LEN), 0) == buckets[...]
    rel_col = jnp.sum(jnp.where(eye, rel[pl.ds(c, 1), :], 0.0), axis=1, keepdims=True)
    relative = jnp.sum(jnp.where(onehot, rel_col, 0.0), axis=0, keepdims=True)
    row8 = lax.broadcasted_iota(jnp.int32, (8, 2 * TB), 0)
    for m in range(nt):
        low = relative[:, m * TB : (m + 1) * TB]
        before = relative[:, (m - 1) * TB : m * TB] if m else low
        x = jnp.broadcast_to(jnp.concatenate([low, before], 1), (8, 2 * TB))
        for bit in (1, 2, 4):
            x = jnp.where((row8 & bit) != 0, pltpu.roll(x, bit, 1), x)
        size = 8
        while size < TB:
            x = jnp.concatenate([x, pltpu.roll(x, size, 1)], 0)
            size *= 2
        toep[m] = x[:, :TB]

    def in_wait(which):
        def step(o, _):
            ref = in_recv.at[which, pl.ds(pl.multiple_of(o * W, W), W)]
            remote(ref, ref, s_in.at[0], r_in.at[which * H + o], (k, c)).wait_recv()
            return 0

        lax.fori_loop(0, H, step, 0)

    user_len = lengths[assign[k]]

    for which in (1, 2, 3):
        in_wait(which)
    for r in range(H):
        vt[:, r * W : (r + 1) * W] = (
            in_recv[1, r * W : (r + 1) * W].astype(jnp.float32).T.astype(jnp.bfloat16)
        )

    key_at = lax.broadcasted_iota(jnp.int32, (TB, TB), 0)
    for ib in range(nt):
        query_at = lax.broadcasted_iota(jnp.int32, (1, TB), 1) + ib * TB
        limit = jnp.where(query_at < user_len, query_at, -1)
        q = in_recv[2, ib * TB : (ib + 1) * TB]
        acc = jnp.zeros((W, TB), jnp.float32)
        for jb in range(ib + 1):
            t = tile_at(ib, jb)
            score = mm(in_recv[3, jb * TB : (jb + 1) * TB], q, NT) + toep[ib - jb]
            live = key_at <= limit - jb * TB
            sig = 0.5 + 0.5 * jnp.tanh(0.5 * score)
            weight = score * sig
            slope = sig + weight * (1.0 - sig)
            wb = jnp.where(live, weight, 0.0).astype(jnp.bfloat16)
            wts[t] = wb
            dsl[t] = jnp.where(live, slope, 0.0)
            acc = acc + mm(vt[:, jb * TB : (jb + 1) * TB], wb, NN)
        at[:, ib * TB : (ib + 1) * TB] = acc

    in_wait(0)

    def cot_wait(o, _):
        cc = lax.rem(c + o, H)
        ref = cot_recv.at[pl.ds(pl.multiple_of(cc * W, W), W)]
        remote(ref, ref, s_cot.at[0], r_cot.at[cc], (k, cc)).wait_recv()
        return 0

    lax.fori_loop(1, H, cot_wait, 0)

    means, spreads, gsums, gdots = [], [], [], []
    for r in range(H):
        rows = slice(r * W, (r + 1) * W)
        up = in_recv[0, rows].astype(jnp.float32).T
        grad = cot_recv[rows].astype(jnp.float32).T * up
        ut[:, rows] = up
        gt[:, rows] = grad
        a = at[:, rows]
        mean = jnp.sum(a, axis=0, keepdims=True) * (1.0 / W)
        centered = a - mean
        means.append(mean)
        spreads.append(jnp.sum(centered * centered, axis=0, keepdims=True))
        gsums.append(jnp.sum(grad, axis=0, keepdims=True))
        gdots.append(jnp.sum(grad * centered, axis=0, keepdims=True))
    for n, rows_of in enumerate((means, spreads, gsums, gdots)):
        st_send[n] = jnp.concatenate(rows_of, 0)

    def st_copy(o):
        cc = lax.rem(c + o, H)
        return remote(st_send, st_recv.at[c], s_st.at[o], r_st.at[c], (k, cc))

    def st_start(o, _):
        st_copy(o).start()
        return 0

    lax.fori_loop(1, H, st_start, 0)
    st_recv[c] = st_send[...]
    for r in range(H):
        kt[:, r * W : (r + 1) * W] = (
            in_recv[3, r * W : (r + 1) * W].astype(jnp.float32).T.astype(jnp.bfloat16)
        )

    def st_wait(o, _):
        cc = lax.rem(c + o, H)
        ref = st_recv.at[cc]
        remote(ref, ref, s_st.at[0], r_st.at[cc], (k, cc)).wait_recv()
        return 0

    lax.fori_loop(1, H, st_wait, 0)

    D = H * W
    mean = st_recv[0, 0]
    for h in range(1, H):
        mean = mean + st_recv[h, 0]
    mean = mean * (1.0 / H)
    square = jnp.zeros_like(mean)
    g_total = jnp.zeros_like(mean)
    gn_total = jnp.zeros_like(mean)
    for h in range(H):
        off = st_recv[h, 0] - mean
        square = square + (st_recv[h, 1] + W * (off * off))
        g_total = g_total + st_recv[h, 2]
        gn_total = gn_total + (st_recv[h, 3] + off * st_recv[h, 2])
    inv = lax.rsqrt(square * (1.0 / D) + 1e-05)
    g_mean = g_total * (1.0 / D)
    gn_mean = gn_total * inv * (1.0 / D)
    for r in range(H):
        rows = slice(r * W, (r + 1) * W)
        row = slice(r, r + 1)
        normed = (at[:, rows] - mean[row]) * inv[row]
        dat[:, rows] = (
            (gt[:, rows] - g_mean[row] - normed * gn_mean[row]) * inv[row]
        ).astype(jnp.bfloat16)
        natural = normed.T
        up = in_recv[0, rows].astype(jnp.float32)
        out_send[rows] = (natural * up).astype(jnp.bfloat16)
        g_send[0, rows] = (natural * cot_recv[rows].astype(jnp.float32)).astype(jnp.bfloat16)

    def g_copy(which, o):
        cc = lax.rem(c + o, H)
        return remote(
            g_send.at[which, pl.ds(pl.multiple_of(cc * W, W), W)],
            g_recv.at[k],
            s_g.at[which * H + o],
            r_g.at[k],
            (which * H + c, cc),
        )

    def g_start(which):
        mine = which * H + c == k

        @pl.when(jnp.logical_not(mine))
        def _():
            g_copy(which, 0).start()

        @pl.when(mine)
        def _():
            pltpu.make_async_copy(
                g_send.at[which, pl.ds(pl.multiple_of(c * W, W), W)], g_recv.at[k], r_g.at[k]
            ).start()

        def step(o, _):
            g_copy(which, o).start()
            return 0

        lax.fori_loop(1, H, step, 0)

    def out_copy(o):
        cc = lax.rem(c + o, H)
        return remote(
            out_send.at[pl.ds(pl.multiple_of(cc * W, W), W)],
            out.at[:, pl.ds(pl.multiple_of(c * W, W), W)],
            s_out.at[o],
            r_out.at[c],
            (k, cc),
        )

    def out_start(o, _):
        out_copy(o).start()
        return 0

    g_start(0)
    lax.fori_loop(1, H, out_start, 0)
    out[:, pl.ds(pl.multiple_of(c * W, W), W)] = out_send[pl.ds(pl.multiple_of(c * W, W), W), :]

    for jb in range(nt):
        acc = jnp.zeros((TB, W), jnp.float32)
        for ib in range(jb, nt):
            acc = acc + mm(wts[tile_at(ib, jb)], dat[:, ib * TB : (ib + 1) * TB], NT)
        g_send[1, jb * TB : (jb + 1) * TB] = acc.astype(jnp.bfloat16)
    g_start(1)

    q_acc = [jnp.zeros((W, TB), jnp.float32) for _ in range(nt)]
    for jb in range(nt):
        value = in_recv[1, jb * TB : (jb + 1) * TB]
        acc = jnp.zeros((TB, W), jnp.float32)
        for ib in range(jb, nt):
            t = tile_at(ib, jb)
            ds = mm(value, dat[:, ib * TB : (ib + 1) * TB], NN) * dsl[t]
            if jb == 0:
                diag[ib - jb] = ds
            else:
                diag[ib - jb] += ds
            dsb = ds.astype(jnp.bfloat16)
            acc = acc + mm(dsb, in_recv[2, ib * TB : (ib + 1) * TB], NN)
            q_acc[ib] = q_acc[ib] + mm(kt[:, jb * TB : (jb + 1) * TB], dsb, NN)
        g_send[3, jb * TB : (jb + 1) * TB] = acc.astype(jnp.bfloat16)
    g_start(3)
    for ib in range(nt):
        for p in range(per):
            r = ib * per + p
            g_send[2, r * W : (r + 1) * W] = (
                q_acc[ib][:, p * W : (p + 1) * W].T.astype(jnp.bfloat16)
            )
    g_start(2)

    sheared = []
    for m in range(nt):
        x = jnp.concatenate([diag[m], jnp.zeros((TB, TB), jnp.float32)], 1)
        size = TB
        while size > 8:
            size //= 2
            x = x[:size] + pltpu.roll(x[size:], 2 * TB - size, 1)
        for bit in (1, 2, 4):
            x = jnp.where((row8 & bit) != 0, pltpu.roll(x, 2 * TB - bit, 1), x)
        sheared.append(jnp.sum(x, axis=0, keepdims=True))
    by_distance = []
    for m in range(nt):
        part = sheared[m][:, :TB]
        if m + 1 < nt:
            part = part + sheared[m + 1][:, TB:]
        by_distance.append(part)
    by_distance = jnp.concatenate(by_distance, 1)
    db_col = jnp.sum(jnp.where(onehot, by_distance, 0.0), axis=1, keepdims=True)
    db_send[0] = jnp.sum(jnp.where(eye, db_col, 0.0), axis=0, keepdims=True)

    def db_dev(o):
        return lax.div(o, H) * H + c, lax.rem(o, H)

    def db_start(o, _):
        kk, cc = db_dev(o)

        @pl.when(jnp.logical_not(jnp.logical_and(kk == k, cc == c)))
        def _():
            remote(db_send.at[0], db_recv.at[k], s_db.at[o], r_db.at[k], (kk, cc)).start()

        return 0

    lax.fori_loop(0, 4 * H, db_start, 0)

    @pl.when(own)
    def _():
        db_recv[k] = db_send[0]

    def db_wait(o, _):
        d = lax.rem(k + o, U)

        @pl.when(jnp.logical_not(jnp.logical_and(o == 0, own)))
        def _():
            ref = db_recv.at[d]
            remote(ref, ref, s_db.at[0], r_db.at[d], (d, e)).wait_recv()

        return 0

    lax.fori_loop(0, U, db_wait, 0)
    db_sum[0] = jnp.sum(db_recv[...], axis=0)

    def dba_start(cc, _):
        kk = comp * H + c

        @pl.when(jnp.logical_not(jnp.logical_and(kk == k, cc == c)))
        def _():
            remote(db_sum.at[0], db_all.at[e], s_dba.at[cc], r_dba.at[e], (kk, cc)).start()

        return 0

    lax.fori_loop(0, H, dba_start, 0)

    @pl.when(own)
    def _():
        db_all[e] = db_sum[0]

    def dba_wait(j, _):
        @pl.when(jnp.logical_not(jnp.logical_and(j == e, own)))
        def _():
            ref = db_all.at[j]
            remote(ref, ref, s_dba.at[0], r_dba.at[j], (comp * H + j, e)).wait_recv()

        return 0

    lax.fori_loop(0, H, dba_wait, 0)
    for j in range(H):
        dbias[j : j + 1, :] = db_all[j]

    def g_wait(d, _):
        ref = g_recv.at[d]
        remote(ref, ref, s_g.at[0], r_g.at[d], (d, e)).wait_recv()
        return 0

    lax.fori_loop(0, U, g_wait, 0)

    def place(u, _):
        grads[u] = g_recv[inverse[u]]
        return 0

    lax.fori_loop(0, U, place, 0)

    def out_wait(o, _):
        cc = lax.rem(c + o, H)
        ref = out.at[:, pl.ds(pl.multiple_of(cc * W, W), W)]
        remote(ref, ref, s_out.at[0], r_out.at[cc], (k, cc)).wait_recv()
        return 0

    lax.fori_loop(1, H, out_wait, 0)

    @pl.when(jnp.logical_not(own))
    def _():
        in_copy(0).wait_send()

    def in_left(o, _):
        in_copy(o).wait_send()
        return 0

    lax.fori_loop(1, U, in_left, 0)

    def ctx_left(o, _):
        cot_copy(o).wait_send()
        st_copy(o).wait_send()
        out_copy(o).wait_send()
        for which in range(4):
            g_copy(which, o).wait_send()
        return 0

    lax.fori_loop(1, H, ctx_left, 0)
    for which in range(4):

        @pl.when(which * H + c != k)
        def _(which=which):
            g_copy(which, 0).wait_send()

    def db_left(o, _):
        kk, cc = db_dev(o)

        @pl.when(jnp.logical_not(jnp.logical_and(kk == k, cc == c)))
        def _():
            remote(db_send.at[0], db_recv.at[k], s_db.at[o], r_db.at[k], (kk, cc)).wait_send()

        return 0

    lax.fori_loop(0, 4 * H, db_left, 0)

    def dba_left(cc, _):
        kk = comp * H + c

        @pl.when(jnp.logical_not(jnp.logical_and(kk == k, cc == c)))
        def _():
            remote(db_sum.at[0], db_all.at[e], s_dba.at[cc], r_dba.at[e], (kk, cc)).wait_send()

        return 0

    lax.fori_loop(0, H, dba_left, 0)


def on_device(uvqk, lengths, assignment, buckets, rel_bias, cotangent):
    U = assignment.shape[0]
    H = rel_bias.shape[0]
    LEN = buckets.shape[0]
    D = H * W
    nt = LEN // TB
    tiles = nt * (nt + 1) // 2
    users = jnp.arange(U, dtype=jnp.int32)
    inverse = jnp.sum(jnp.where(assignment[None, :] == users[:, None], users[None, :], 0), axis=1)
    vm = pl.BlockSpec(memory_space=pltpu.VMEM)
    sm = pl.BlockSpec(memory_space=pltpu.SMEM)
    bf, f32 = jnp.bfloat16, jnp.float32
    dma = pltpu.SemaphoreType.DMA
    out, grads, dbias = pl.pallas_call(
        functools.partial(kernel, H, U),
        out_shape=[
            jax.ShapeDtypeStruct((W, D), bf),
            jax.ShapeDtypeStruct((U, W, W), bf),
            jax.ShapeDtypeStruct((H, W), f32),
        ],
        in_specs=[sm, sm, sm, vm, vm, vm, vm],
        out_specs=[vm, vm, vm],
        scratch_shapes=[
            pltpu.VMEM((U, W, W), bf),
            pltpu.VMEM((4, LEN, W), bf),
            pltpu.VMEM((LEN, W), bf),
            pltpu.VMEM((LEN, W), bf),
            pltpu.VMEM((4, LEN, W), bf),
            pltpu.VMEM((U, W, W), bf),
            pltpu.VMEM((nt, TB, TB), f32),
            pltpu.VMEM((tiles, TB, TB), bf),
            pltpu.VMEM((tiles, TB, TB), f32),
            pltpu.VMEM((nt, TB, TB), f32),
            pltpu.VMEM((W, LEN), bf),
            pltpu.VMEM((W, LEN), bf),
            pltpu.VMEM((W, LEN), f32),
            pltpu.VMEM((W, LEN), f32),
            pltpu.VMEM((W, LEN), f32),
            pltpu.VMEM((W, LEN), bf),
            pltpu.VMEM((H, 4, H, W), f32),
            pltpu.VMEM((4, H, W), f32),
            pltpu.VMEM((1, 1, W), f32),
            pltpu.VMEM((U, 1, W), f32),
            pltpu.VMEM((1, 1, W), f32),
            pltpu.VMEM((H, 1, W), f32),
            dma((U,)),
            dma((4 * H,)),
            dma((H,)),
            dma((H,)),
            dma((H,)),
            dma((H,)),
            dma((H,)),
            dma((H,)),
            dma((4 * H,)),
            dma((U,)),
            dma((4 * H,)),
            dma((U,)),
            dma((H,)),
            dma((H,)),
        ],
        compiler_params=pltpu.CompilerParams(
            collective_id=0, has_side_effects=True, vmem_limit_bytes=40 * 1024 * 1024
        ),
        name="layer",
    )(
        assignment,
        inverse,
        lengths,
        uvqk,
        cotangent.reshape(W, D),
        buckets.reshape(1, LEN),
        rel_bias,
    )
    return out.reshape(1, W, D), grads, dbias


def solution(mesh):
    in_specs = (P(None, "ctx", "dp"), P(), P(), P(), P(), P("dp", "ctx", None))
    out_specs = (P("dp", "ctx", None), P(None, "ctx", "dp"), P())
    return jax.shard_map(
        on_device, mesh=mesh, in_specs=in_specs, out_specs=out_specs, check_vma=False
    )
```

time: 369 us -> 103 us (0.28); the launches traced: 363 us -> 103 us
  blocking collectives: 114 us -> 0 us
  Pallas kernels: 0 us -> 96.2 us
  local copies, waits for them, and re-layouts: 86 us -> 5.14 us
  waiting for transfers between devices: 80 us -> 0 us
  other arithmetic: 40.3 us -> 0.82 us
  between operations: 17.2 us -> 0.7 us
  matrix products: 15.4 us -> 0 us
  starting transfers between devices: 9.82 us -> 0 us
    pallas_call x0 -> x1, Pallas kernels: none -> 96.2 us  [on_device(): pl.pallas_call(functools.partial(kernel, H, U), out_shape=[jax.ShapeDtype...]
    psum x1 -> x0, blocking collectives: 76.3 us -> none  [on_device(): d_bias = lax.psum(d_bias, ('dp', 'ctx'))]
    reduce_scatter x1 -> x0, waiting for transfers between devices: 52.9 us -> none  [on_device(): lax.psum_scatter(jnp.concatenate(key_terms, 1), 'ctx', scatter_dimension=...]
    all_to_all x1 -> x0, blocking collectives: 38 us -> none  [on_device(): lax.all_to_all(arranged, 'dp', split_axis=0, concat_axis=2, tiled=True)]
    all_gather x2 -> x0, waiting for transfers between devices: 26.4 us -> none  [the longest x1 26.4 us: on_device(): lax.all_gather(value_part, 'ctx', axis=1, tiled=True)]
    unnamed x1 -> x0, other arithmetic: 23.4 us -> none
    reshape x4 -> x0, local copies, waits for them, and re-layouts: 18.2 us -> none  [the longest x2 9.13 us: diagonal_sums(): return flat.reshape(head_count, rows, columns + rows + 1).sum(1)]
    concatenate x1 -> x0, local copies, waits for them, and re-layouts: 17.1 us -> none  [on_device(): jnp.concatenate([d_up, d_value.astype(jnp.bfloat16), d_query.astype(jnp.b...]
  transfers between devices with their start and end apart: 4 -> 0, of which waited for: 2 -> 0; matrix products, arithmetic and copies ran while one was open for 16% -> 0% of each run, Pallas kernels for 0% -> 0%
where the time goes in v1:
time: 103 us
  Pallas kernels  96.2 us (93%)
  local copies, waits for them, and re-layouts  5.14 us (5%)
    pallas_call x1, Pallas kernels, on_device(): pl.pallas_call(functools.partial(kernel, H, U), out_shape=[jax.ShapeDtype...  96.2 us
    unnamed x15, local copies, waits for them, and re-layouts  5.14 us

profile of v1, /device:TPU:1, one launch (start us, length us, event | category | flops | bytes accessed | tf_op | source)
XLA Modules:
  0.0 102.8 jit_solution(1888448429472860905)
XLA Ops:
  0.6 0.0 copy-start.2
  0.6 0.0 copy-start.4
  0.7 0.0 copy-start.5
  0.7 0.8 select_reduce_fusion.inverse
  1.5 0.0 copy-done.2
  1.5 0.0 copy-done.4
  1.5 0.0 copy-done.5
  1.5 0.0 copy-start
  1.5 1.2 %copy-done = bf16[32,128,128]{2,1,0:T(8,128)(2,1)S(1)} copy-done((bf16[32,128,128]{2,1,0:T(8,128)(2,1)S(1)}, bf16[32,128,128]{2,1,0:T(8,128)(2,1)}, u32[]{:S(2)}) %copy-start) | copy-done | bytes 1048600
  2.7 0.0 copy-start.1
  2.7 0.9 copy-done.1
  3.7 0.0 copy-start.3
  3.7 0.7 copy-done.3
  4.4 96.2 %layer.1 = (bf16[128,1024]{1,0:T(8,128)(2,1)S(1)}, bf16[32,128,128]{2,1,0:T(8,128)(2,1)S(1)}, f32[8,128]{1,0:T(8,128)S(1)}) custom-call(s32[32]{0:T(128)S(1)} %copy-done.4, s32[32]{0:T(128)S(1)} %select_reduce_fusion.inverse, s32[32]{0:T(128)S(1)} %copy-done.5, bf16[32,128,128]{2,1,0:T(8,128)(2,1)S(1)} %copy-done, bf16[128,1024]{1,0:T(8,128)(2,1)S(1)} %bitcast.4, ...), custom_call_target="tpu_custom_call" | custom-call | tf_op jit(solution)/shard_map/layer/pallas_call | solution.py:546
  100.6 0.7 copy.12
  101.3 1.0 copy.13
  102.2 0.6 copy.14
Async XLA Ops:
  0.6 0.9 copy-start.2
  0.6 0.8 copy-start.4
  0.7 0.8 copy-start.5
  1.5 1.2 %copy-start = (bf16[32,128,128]{2,1,0:T(8,128)(2,1)S(1)}, bf16[32,128,128]{2,1,0:T(8,128)(2,1)}, u32[]{:S(2)}) copy-start(bf16[32,128,128]{2,1,0:T(8,128)(2,1)} %uvqk.1) | copy-start | bytes 3145732
  2.7 0.9 copy-start.1
  3.7 0.7 copy-start.3
